TPU v7x, 32 devices: a whole 2x2x4 slice. The times are simulated.
32 devices in a mesh: group: 4 (over y, x), dp: 8 (over z, core).
Axes of the slice: x: 2, y: 2, z: 4, core: 2. Of those that a mesh axis runs over, the one named last changes fastest.
Arguments:
- tokens: bfloat16 [32, 512, 768], P(('group', 'dp')), may hold values from -6 to 6
- cotangent: bfloat16 [32, 512, 768], P(('group', 'dp')), may hold values from -6 to 6
- replay_count: int32 [1], replicated, may hold values from 8 to 16
- row_length: int32 [32], P(('group', 'dp')), may hold values from 106 to 512, as said below
- response_mask: int32 [32, 512], P(('group', 'dp')), may hold values from 0 to 1, as said below
- proj_weight: bfloat16 [768, 2304], replicated, may hold values from -0.21875 to 0.21875
- query_bias: float32 [768], replicated, may hold values from -3 to 3
- value_bias: float32 [768], replicated, may hold values from -3 to 3
- out_weight: bfloat16 [768, 768], replicated, may hold values from -1.75 to 1.75
- out_bias: float32 [768], replicated, may hold values from -2 to 2
- first_gain: float32 [768], replicated, may hold values from 0.1 to 1.9
- first_shift: float32 [768], replicated, may hold values from -2 to 2
- second_gain: float32 [768], replicated, may hold values from 0.1 to 1.9
- second_shift: float32 [768], replicated, may hold values from -2 to 2
- up_weight: bfloat16 [768, 3072], replicated, may hold values from -0.21875 to 0.21875
- up_bias: float32 [3072], replicated, may hold values from -3 to 3
- down_weight: bfloat16 [3072, 768], replicated, may hold values from -0.109375 to 0.109375
- down_bias: float32 [768], replicated, may hold values from -2 to 2
Outputs:
- output: bfloat16 [32, 512, 768], P(('group', 'dp'))
- tokens_grad: float32 [32, 512, 768], P(('group', 'dp'))
- proj_weight_grad: float32 [768, 2304], P('dp')
- query_bias_grad: float32 [768], P('dp')
- value_bias_grad: float32 [768], P('dp')
- out_weight_grad: float32 [768, 768], P('dp')
- out_bias_grad: float32 [768], P('dp')
- first_gain_grad: float32 [768], P('dp')
- first_shift_grad: float32 [768], P('dp')
- second_gain_grad: float32 [768], P('dp')
- second_shift_grad: float32 [768], P('dp')
- up_weight_grad: float32 [768, 3072], P('dp')
- up_bias_grad: float32 [3072], P('dp')
- down_weight_grad: float32 [3072, 768], P('dp')
- down_bias_grad: float32 [768], P('dp')
Inputs may be any that keep to these rules, and one draw needn't show every extreme that they name: `row_length`: positions of a row at or past its length are padding. `response_mask`: zero at positions at or past the row's length; every row has at least one 1.
All inputs are finite; a program needn't handle non-finite values.
Results may differ from a plain program's by a relative error of at most 0.011.
Values sent between devices are 32-bit elements; how exact they have to be, the bound alone decides.
A program may use at most 256 MiB of HBM per device.

v0:
```python
import jax
import jax.numpy as jnp
from jax import lax
from jax.sharding import PartitionSpec as P

HEAD_DIM = 64


eps_norm = 1e-05
masked_score = -1e30


def layer_norm(inputs, gain, shift):
    average = jnp.mean(inputs, axis=-1, keepdims=True)
    centered = inputs - average
    variance = jnp.mean(centered * centered, axis=-1, keepdims=True)
    return centered * lax.rsqrt(variance + eps_norm) * gain + shift


def tanh_gelu(inputs):
    return jax.nn.gelu(inputs, approximate=True)


def plain_product(left, right):
    return jnp.dot(left, right, preferred_element_type=jnp.float32)


def outer_product(left, right):
    return lax.dot_general(
        left, right, (((0,), (0,)), ((), ())), preferred_element_type=jnp.float32
    )


def transposed_product(left, right):
    return lax.dot_general(
        left, right, (((1,), (1,)), ((), ())), preferred_element_type=jnp.float32
    )


def block_scores(query_block, key_heads, row_start, length, score_scale):
    scores = (
        jnp.einsum("qhd,khd->hqk", query_block, key_heads, preferred_element_type=jnp.float32)
        * score_scale
    )
    query_pos = row_start + jnp.arange(query_block.shape[0])
    key_pos = jnp.arange(key_heads.shape[0])
    allowed = (key_pos[None, :] <= query_pos[:, None]) & (key_pos[None, :] < length)
    return jnp.where(allowed[None], scores, masked_score)


def attend_row(query_heads, key_heads, value_heads, length, block_rows, score_scale):

    def one_block(block_index):
        row_start = block_index * block_rows
        scores = block_scores(query_heads, key_heads, row_start, length, score_scale)
        highest = jnp.max(scores, axis=-1, keepdims=True)
        raised = jnp.exp(scores - highest)
        row_total = jnp.sum(raised, axis=-1, keepdims=True)
        prob_table = raised / row_total
        mixed_block = jnp.einsum(
            "hqk,khd->qhd",
            prob_table.astype(jnp.bfloat16),
            value_heads,
            preferred_element_type=jnp.float32,
        )
        return (mixed_block, highest + jnp.log(row_total))

    block_count = query_heads.shape[0] // block_rows
    mixed_blocks, log_total = lax.map(one_block, jnp.arange(block_count))
    return (mixed_blocks.reshape(query_heads.shape), log_total)


def attend_back(
    query_heads, key_heads, value_heads, length, log_total, mixed_grad, block_rows, score_scale
):

    def one_block(running, inputs):
        key_grad, value_grad = running
        block_index, block_log = inputs
        row_start = block_index * block_rows
        scores = block_scores(query_heads, key_heads, row_start, length, score_scale)
        prob_table = jnp.exp(scores - block_log)
        value_grad = value_grad + jnp.einsum(
            "hqk,qhd->khd",
            prob_table.astype(jnp.bfloat16),
            mixed_grad,
            preferred_element_type=jnp.float32,
        )
        prob_grad = jnp.einsum(
            "qhd,khd->hqk", mixed_grad, value_heads, preferred_element_type=jnp.float32
        )
        inner_sum = jnp.sum(prob_grad * prob_table, axis=-1, keepdims=True)
        score_grad = (prob_table * (prob_grad - inner_sum)).astype(jnp.bfloat16)
        query_grad = (
            jnp.einsum("hqk,khd->qhd", score_grad, key_heads, preferred_element_type=jnp.float32)
            * score_scale
        )
        key_grad = (
            key_grad
            + jnp.einsum(
                "hqk,qhd->khd", score_grad, query_heads, preferred_element_type=jnp.float32
            )
            * score_scale
        )
        return ((key_grad, value_grad), query_grad)

    zero_grads = jnp.zeros(key_heads.shape, jnp.float32)
    block_count = query_heads.shape[0] // block_rows
    (key_grad, value_grad), query_grad = lax.scan(
        one_block, (zero_grads, zero_grads), (jnp.arange(block_count), log_total)
    )
    return (query_grad.reshape(query_heads.shape), key_grad, value_grad)


def shards(
    tokens,
    cotangent,
    replay_count,
    row_length,
    response_mask,
    proj_weight,
    query_bias,
    value_bias,
    out_weight,
    out_bias,
    first_gain,
    first_shift,
    second_gain,
    second_shift,
    up_weight,
    up_bias,
    down_weight,
    down_bias,
):
    group_size = lax.axis_size("group")
    dp_size = lax.axis_size("dp")
    local_rows, token_count, model_width = tokens.shape
    head_count = model_width // HEAD_DIM
    score_scale = HEAD_DIM ** (-0.5)
    block_rows = min(512, token_count)
    head_shape = (local_rows, token_count, head_count, HEAD_DIM)
    first_row = (lax.axis_index("group") * dp_size + lax.axis_index("dp")) * local_rows
    row_ids = first_row + jnp.arange(local_rows)
    replay_rows = local_rows * dp_size * (group_size // 2)
    is_replay = lax.axis_index("group") < group_size // 2
    in_use = jnp.where(is_replay, row_ids < replay_count[0], True)
    live_tokens = (response_mask * in_use[:, None].astype(jnp.int32)).astype(jnp.float32)
    own_total = jnp.sum(live_tokens)
    count_terms = jnp.stack(
        [jnp.where(is_replay, own_total, 0.0), jnp.where(is_replay, 0.0, own_total)]
    )
    totals = lax.psum(count_terms, ("group", "dp"))
    slots = float(replay_rows * token_count)
    row_scale = jnp.where(is_replay, slots / totals[0], slots / totals[1])
    token_weight = live_tokens * row_scale
    flat_in = tokens.reshape(-1, model_width).astype(jnp.float32)
    first_norm, first_back = jax.vjp(layer_norm, flat_in, first_gain, first_shift)
    normed_low = first_norm.astype(jnp.bfloat16)
    projected = plain_product(normed_low, proj_weight)
    query_heads = (projected[:, :model_width] + query_bias).astype(jnp.bfloat16).reshape(head_shape)
    key_heads = projected[:, model_width : 2 * model_width].astype(jnp.bfloat16).reshape(head_shape)
    value_heads = (
        (projected[:, 2 * model_width :] + value_bias).astype(jnp.bfloat16).reshape(head_shape)
    )

    def forward_row(row_inputs):
        query_row, key_row, value_row, length = row_inputs
        return attend_row(query_row, key_row, value_row, length, block_rows, score_scale)

    mixed_heads, log_total = lax.map(forward_row, (query_heads, key_heads, value_heads, row_length))
    mixed_low = mixed_heads.reshape(-1, model_width).astype(jnp.bfloat16)
    attn_out = plain_product(mixed_low, out_weight) + out_bias
    residual = flat_in + attn_out
    second_norm, second_back = jax.vjp(layer_norm, residual, second_gain, second_shift)
    second_low = second_norm.astype(jnp.bfloat16)
    hidden = plain_product(second_low, up_weight) + up_bias
    activated, gelu_back = jax.vjp(tanh_gelu, hidden)
    activated_low = activated.astype(jnp.bfloat16)
    branch = plain_product(activated_low, down_weight) + down_bias
    output = (residual + branch).astype(jnp.bfloat16).reshape(tokens.shape)
    out_grad = cotangent.reshape(-1, model_width).astype(jnp.float32) * token_weight.reshape(-1, 1)
    branch_low = out_grad.astype(jnp.bfloat16)
    down_weight_grad = outer_product(activated_low, branch_low)
    down_bias_grad = jnp.sum(branch_low, axis=0, dtype=jnp.float32)
    activated_grad = transposed_product(branch_low, down_weight)
    (hidden_grad,) = gelu_back(activated_grad)
    hidden_low = hidden_grad.astype(jnp.bfloat16)
    up_weight_grad = outer_product(second_low, hidden_low)
    up_bias_grad = jnp.sum(hidden_low, axis=0, dtype=jnp.float32)
    second_grad = transposed_product(hidden_low, up_weight)
    residual_part, second_gain_grad, second_shift_grad = second_back(second_grad)
    residual_grad = out_grad + residual_part
    attn_low = residual_grad.astype(jnp.bfloat16)
    out_weight_grad = outer_product(mixed_low, attn_low)
    out_bias_grad = jnp.sum(attn_low, axis=0, dtype=jnp.float32)
    mixed_grad = transposed_product(attn_low, out_weight).astype(jnp.bfloat16).reshape(head_shape)

    def backward_row(row_inputs):
        query_row, key_row, value_row, length, row_log, grad_row = row_inputs
        return attend_back(
            query_row, key_row, value_row, length, row_log, grad_row, block_rows, score_scale
        )

    query_grad, key_grad, value_grad = lax.map(
        backward_row, (query_heads, key_heads, value_heads, row_length, log_total, mixed_grad)
    )
    query_low = query_grad.reshape(-1, model_width).astype(jnp.bfloat16)
    key_low = key_grad.reshape(-1, model_width).astype(jnp.bfloat16)
    value_low = value_grad.reshape(-1, model_width).astype(jnp.bfloat16)
    proj_grad_low = jnp.concatenate([query_low, key_low, value_low], axis=1)
    proj_weight_grad = outer_product(normed_low, proj_grad_low)
    query_bias_grad = jnp.sum(query_low, axis=0, dtype=jnp.float32)
    value_bias_grad = jnp.sum(value_low, axis=0, dtype=jnp.float32)
    first_grad = transposed_product(proj_grad_low, proj_weight)
    input_part, first_gain_grad, first_shift_grad = first_back(first_grad)
    tokens_grad = (residual_grad + input_part).reshape(tokens.shape)
    shares = (
        lax.psum_scatter(proj_weight_grad, "dp", scatter_dimension=0, tiled=True),
        lax.psum_scatter(query_bias_grad, "dp", scatter_dimension=0, tiled=True),
        lax.psum_scatter(value_bias_grad, "dp", scatter_dimension=0, tiled=True),
        lax.psum_scatter(out_weight_grad, "dp", scatter_dimension=0, tiled=True),
        lax.psum_scatter(out_bias_grad, "dp", scatter_dimension=0, tiled=True),
        lax.psum_scatter(first_gain_grad, "dp", scatter_dimension=0, tiled=True),
        lax.psum_scatter(first_shift_grad, "dp", scatter_dimension=0, tiled=True),
        lax.psum_scatter(second_gain_grad, "dp", scatter_dimension=0, tiled=True),
        lax.psum_scatter(second_shift_grad, "dp", scatter_dimension=0, tiled=True),
        lax.psum_scatter(up_weight_grad, "dp", scatter_dimension=0, tiled=True),
        lax.psum_scatter(up_bias_grad, "dp", scatter_dimension=0, tiled=True),
        lax.psum_scatter(down_weight_grad, "dp", scatter_dimension=0, tiled=True),
        lax.psum_scatter(down_bias_grad, "dp", scatter_dimension=0, tiled=True),
    )
    summed = lax.psum(tuple(shares), "group")
    pieces = tuple(summed)
    return (output, tokens_grad) + pieces


def solution(mesh):
    in_specs = (
        P(("group", "dp"), None, None),
        P(("group", "dp"), None, None),
        P(),
        P(("group", "dp")),
        P(("group", "dp"), None),
        P(),
        P(),
        P(),
        P(),
        P(),
        P(),
        P(),
        P(),
        P(),
        P(),
        P(),
        P(),
        P(),
    )
    out_specs = (
        P(("group", "dp"), None, None),
        P(("group", "dp"), None, None),
        P("dp", None),
        P("dp"),
        P("dp"),
        P("dp", None),
        P("dp"),
        P("dp"),
        P("dp"),
        P("dp"),
        P("dp"),
        P("dp", None),
        P("dp"),
        P("dp", None),
        P("dp"),
    )
    return jax.shard_map(shards, mesh=mesh, in_specs=in_specs, out_specs=out_specs, check_vma=False)
```

profile of v0, /device:TPU:0, one launch (start us, length us, event | category | flops | bytes accessed | tf_op | source)
XLA Modules:
  0.0 540.3 jit_solution(1424592745422267185)
XLA Ops:
  8.0 1.5 convert_reduce_fusion.6
  11.6 42.0 %psum.98 = f32[2]{0:T(128)S(1)} all-reduce(f32[2]{0:T(128)S(1)} %pad_maximum_fusion.3), channel_id=1, replica_groups=mesh['group'=4,'dp'=8] {'group','dp'}, use_global_device_ids=true, to_apply=%region_7.8 | all-reduce | flops 2 | bytes 16 | tf_op jit(solution)/shard_map/psum | solution.py:152
  56.1 0.7 convert_multiply_fusion.1
  56.8 1.3 convert_reduce_fusion.1
  58.1 1.5 fusion.25
  59.6 1.5 fusion.36
  61.1 3.3 fusion.55
  64.5 1.0 slice.31
  65.4 1.4 fusion.27
  66.8 2.3 copy.54
  69.1 2.4 copy.55
  71.5 2.3 copy.53
  73.8 3.5 fusion.13
  77.3 3.7 fusion
  81.0 0.8 copy-done.1
  81.8 4.9 fusion.34
  86.8 0.9 fusion.64
  88.2 5.7 %fusion.59 = f32[512,3072]{1,0:T(8,128)S(1)} fusion(bf16[768,3072]{1,0:T(8,128)(2,1)} %param.32, f32[512,768]{1,0:T(8,128)S(1)} %get-tuple-element.175, f32[768]{0:T(1024)S(1)} %copy-done.42, f32[768]{0:T(1024)S(1)} %copy-done.36, f32[512]{0:T(512)S(1)} %fusion.41, f32[512]{0:T(512)S(1)} %broadcast_multiply_fusion), kind=kOutput, calls=%fused_computation.96 | convolution fusion | flops 2417885184 | bytes 12593152 | tf_op jit(solution)/shard_map/dot_general | solution.py:25
  94.0 8.7 %convert_reduce_fusion = (f32[3072]{0:T(1024)}, bf16[512,3072]{1,0:T(8,128)(2,1)S(1)}) fusion(f32[512,3072]{1,0:T(8,128)S(1)} %fusion.59, f32[3072]{0:T(1024)S(1)} %copy-done.38, bf16[3072,768]{1,0:T(8,128)(2,1)S(1)} %bitcast.128, bf16[1,512,768]{2,1,0:T(8,128)(2,1)S(1)} %copy-done.13, f32[512]{0:T(512)S(1)} %bitcast.121), kind=kOutput, calls=%fused_computation.18 | convolution fusion | flops 2453271552 | bytes 14968832 | tf_op jit(solution)/shard_map/dot_general | solution.py:35
  102.8 3.5 multiply_reduce_fusion.1
  106.3 0.7 fusion.62
  107.0 1.1 copy-done.2
  108.1 1.0 convert_reduce_fusion.3
  109.1 0.9 copy-done.14
  110.0 2.2 fusion.65
  112.3 3.2 convolution_convert_fusion
  115.6 0.6 log_add_fusion
  116.2 2.3 copy.57
  118.5 13.5 %multiply_reduce_fusion = (f32[12,512]{1,0:T(8,128)S(1)}, f32[12,512,512]{1,2,0:T(8,128)}) fusion(f32[12,512]{1,0:T(8,128)} %log_add_fusion, f32[12,512,512]{1,2,0:T(8,128)} %copy-done.1, pred[512,512]{0,1:T(8,128)(4,1)} %fusion.36, bf16[512,12,64]{0,2,1:T(8,128)(2,1)} %bitcast.113, bf16[512,12,64]{0,2,1:T(8,128)(2,1)} %bitcast.112), kind=kOutput, calls=%fused_computation.1 | convolution fusion | flops 418375680 | bytes 27049984 | tf_op jit(solution)/shard_map/while/body/eval_jaxpr/while/body/eval_jaxpr/qhd,khd->hqk/dot_general | solution.py:89
  132.0 7.3 %multiply_convert_fusion = bf16[12,512,512]{1,2,0:T(8,128)(2,1)S(1)} fusion(f32[12,512,512]{1,2,0:T(8,128)} %get-tuple-element.178, f32[12,512]{1,0:T(8,128)S(1)} %get-tuple-element.177, f32[12,512]{1,0:T(8,128)S(1)} %copy-done.21, f32[12,512,512]{1,2,0:T(8,128)S(1)} %bitcast.106, pred[512,512]{0,1:T(8,128)(4,1)S(1)} %copy-done.8), kind=kLoop, calls=%fused_computation | loop fusion | flops 18874368 | bytes 31768576 | tf_op jit(solution)/shard_map/while/body/eval_jaxpr/while/body/eval_jaxpr/convert_element_type | solution.py:93
  139.4 2.9 multiply_convert_fusion.2
  142.3 1.2 convert_reduce_fusion.5
  143.5 3.9 convert_reduce_fusion.4
  147.5 0.9 copy-done.44
  148.4 5.3 fusion.37
  153.7 10.2 %fusion.48 = f32[3072,768]{1,0:T(8,128)} fusion(bf16[1,512,768]{2,1,0:T(8,128)(2,1)} %param.19, f32[512]{0:T(512)S(1)} %bitcast.123, f32[512,3072]{1,0:T(8,128)} %copy-done.45, f32[3072]{0:T(1024)} %param.33), kind=kOutput, calls=%fused_computation.91 | convolution fusion | flops 2432827392 | bytes 16529408 | tf_op jit(solution)/shard_map/dot_general | solution.py:29
  164.2 8.9 %fusion.58 = f32[768,3072]{1,0:T(8,128)} fusion(bf16[512,3072]{1,0:T(8,128)(2,1)} %copy-done.46, f32[512,768]{1,0:T(8,128)} %copy-done.9, f32[768]{0:T(1024)} %param.31, f32[768]{0:T(1024)} %param.30, f32[512]{0:T(512)} %copy-done.33, f32[512]{0:T(512)} %copy-done.28), kind=kOutput, calls=%fused_computation.95 | convolution fusion | flops 2417885184 | bytes 14166016 | tf_op jit(solution)/shard_map/dot_general | solution.py:29
  173.3 57.7 %reduce-scatter.5.cloned.1.call-done = f32[96,2304]{1,0:T(8,128)} async-done(((f32[768,2304]{1,0:T(8,128)}), f32[96,2304]{1,0:T(8,128)}) %reduce-scatter.5.cloned.1.call-update) | async-done | bytes 884752 | tf_op jit(solution)/shard_map/reduce_scatter | solution.py:218
  231.0 100.2 %reduce-scatter.11.cloned.1.call-done = f32[384,768]{1,0:T(8,128)} async-done(((f32[3072,768]{1,0:T(8,128)}), f32[384,768]{1,0:T(8,128)}) %reduce-scatter.11.cloned.1.call-update) | async-done | bytes 1179664 | tf_op jit(solution)/shard_map/reduce_scatter | solution.py:229
  331.2 100.1 %reduce-scatter.9.cloned.1.call-done = f32[96,3072]{1,0:T(8,128)} async-done(((f32[768,3072]{1,0:T(8,128)}), f32[96,3072]{1,0:T(8,128)}) %reduce-scatter.9.cloned.1.call-update) | async-done | bytes 1179664 | tf_op jit(solution)/shard_map/reduce_scatter | solution.py:227
  431.3 1.2 dynamic-slice.1
  433.8 1.4 reduce_sum.234
  435.2 0.7 reduce_sum.232
  435.9 4.8 fusion.60
  440.7 1.4 fusion.24
  442.1 27.5 %all-reduce.9 = (f32[768]{0:T(1024)}, f32[768]{0:T(1024)}, f32[768]{0:T(1024)}, f32[768]{0:T(1024)}, f32[768]{0:T(1024)}, /*index=5*/f32[768]{0:T(1024)}, f32[768]{0:T(1024)}, f32[3072]{0:T(1024)}, f32[768]{0:T(1024)}) all-reduce(f32[768]{0:T(1024)} %reduce_sum.232, ...), channel_id=3, replica_groups=mesh['group'=4,'dp'=8] {'dp'}, use_global_device_ids=true, to_apply=%region_16.17.clone | all-reduce | flops 9216 | bytes 73728
  469.6 1.3 dynamic-slice.2
  470.9 1.3 dynamic-slice.4
  472.2 1.3 dynamic-slice.6
  473.4 1.3 dynamic-slice.8
  474.7 1.3 dynamic-slice.10
  476.0 1.3 dynamic-slice.12
  477.2 1.3 dynamic-slice.14
  478.5 1.3 dynamic-slice.18
  479.8 1.3 dynamic-slice.16
  481.1 10.9 %all-reduce.10 = (f32[96]{0:T(128)}, f32[96]{0:T(128)}, f32[96]{0:T(128)}, f32[96]{0:T(128)}, f32[96]{0:T(128)}, /*index=5*/f32[96]{0:T(128)}, f32[96]{0:T(128)}, f32[384]{0:T(512)}, f32[96]{0:T(128)}) all-reduce(f32[96]{0:T(128)} %dynamic-slice.2, f32[96]{0:T(128)} %dynamic-slice.4, ...), channel_id=1, replica_groups=mesh['group'=4,'dp'=8] {'group'}, use_global_device_ids=true, to_apply=%region_17.18 | all-reduce | flops 1152 | bytes 9216 | tf_op jit(solution)/shard_map/psum | solution.py:232
  492.0 0.7 negate_multiply_fusion
  492.6 3.8 add_bitcast_fusion
  496.4 9.0 %fusion.35 = bf16[1,512,768]{2,1,0:T(8,128)(2,1)} fusion(f32[512,768]{1,0:T(8,128)S(1)} %copy-done.10, bf16[3072,768]{1,0:T(8,128)(2,1)} %param.34, f32[768]{0:T(1024)S(1)} %copy-done.43, f32[512,3072]{1,0:T(8,128)} %copy-done.45, f32[3072]{0:T(1024)S(1)} %copy-done.39), kind=kOutput, calls=%fused_computation.64 | convolution fusion | flops 2432827392 | bytes 13384704 | tf_op jit(solution)/shard_map/dot_general | solution.py:25
  505.4 21.9 %all-reduce.14.cloned.1.call-done = (f32[96,2304]{1,0:T(8,128)}, f32[96,768]{1,0:T(8,128)}, f32[96,3072]{1,0:T(8,128)}, f32[384,768]{1,0:T(8,128)}) async-done(((f32[96,2304]{1,0:T(8,128)}, f32[96,768]{1,0:T(8,128)}, f32[96,3072]{1,0:T(8,128)}, f32[384,768]{1,0:T(8,128)}), (f32[96,2304]{1,0:T(8,128)}, f32[96,768]{1,0:T(8,128)}, f32[96,3072]{1,0:T(8,128)}, ...) | async-done | bytes 3538960 | tf_op jit(solution)/shard_map/psum | solution.py:232
  527.3 2.3 copy.71
  529.6 1.7 copy.72
  531.3 1.0 copy.73
  532.3 1.0 copy.74
  (129 shorter events, 2.3 us)
Async XLA Ops:
  7.2 53.9 %copy-start = (bf16[768,2304]{1,0:T(8,128)(2,1)S(1)}, bf16[768,2304]{1,0:T(8,128)(2,1)}, u32[]{:S(2)}) copy-start(bf16[768,2304]{1,0:T(8,128)(2,1)} %param.23) | copy-start | bytes 10616836
  7.2 166.1 %reduce-scatter.7.cloned.1.call-start = ((), (), s32[]{:S(2)}) async-start(), calls=%async_computation.5 | async-start | bytes 2654208 | tf_op jit(solution)/shard_map/reduce_scatter | solution.py:221
  59.6 4.9 copy-start.29
  59.6 4.9 copy-start.24
  61.1 4.3 copy-start.34
  61.1 4.3 copy-start.35
  77.3 4.5 copy-start.1
  77.3 4.5 copy-start.19
  81.0 5.7 %copy-start.22 = (f32[12,512]{1,0:T(8,128)}, f32[12,512]{1,0:T(8,128)S(1)}, u32[]{:S(2)}) copy-start(f32[12,512]{1,0:T(8,128)S(1)} %fusion) | copy-start | bytes 73732
  81.8 4.9 copy-start.3
  81.8 4.9 copy-start.37
  81.8 5.0 copy-start.40
  86.8 1.3 copy-start.36
  86.8 1.3 copy-start.42
  87.7 18.6 %copy-start.9 = (f32[512,768]{1,0:T(8,128)}, f32[512,768]{1,0:T(8,128)S(1)}, u32[]{:S(2)}) copy-start(f32[512,768]{1,0:T(8,128)S(1)} %get-tuple-element.175) | copy-start | bytes 4718596
  87.7 18.6 %copy-start.28 = (f32[512]{0:T(512)}, f32[512]{0:T(512)S(1)}, u32[]{:S(2)}) copy-start(f32[512]{0:T(512)S(1)} %broadcast_multiply_fusion) | copy-start | bytes 6148
  87.8 6.2 %slice-start.5 = ((s8[4718592]{0:T(1024)(128)(4,1)}), s8[4194304]{0:T(1024)(128)(4,1)S(1)}, s32[]{:S(2)}) async-start(s8[4718592]{0:T(1024)(128)(4,1)} %bitcast.127), calls=%async_computation.14 | async-start | bytes 8388608
  88.1 18.2 %copy-start.33 = (f32[512]{0:T(512)}, f32[512]{0:T(512)S(1)}, u32[]{:S(2)}) copy-start(f32[512]{0:T(512)S(1)} %fusion.41) | copy-start | bytes 6148
  88.1 5.8 %copy-start.13 = (bf16[1,512,768]{2,1,0:T(8,128)(2,1)S(1)}, bf16[1,512,768]{2,1,0:T(8,128)(2,1)}, u32[]{:S(2)}) copy-start(bf16[1,512,768]{2,1,0:T(8,128)(2,1)} %param.19) | copy-start | bytes 2359300
  88.1 5.8 %slice-start.6 = ((s8[4718592]{0:T(1024)(128)(4,1)}), s8[524288]{0:T(1024)(128)(4,1)S(1)}, s32[]{:S(2)}) async-start(s8[4718592]{0:T(1024)(128)(4,1)} %bitcast.127), calls=%async_computation.15 | async-start | bytes 1048576
  88.1 5.8 %copy-start.38 = (f32[3072]{0:T(1024)S(1)}, f32[3072]{0:T(1024)}, u32[]{:S(2)}) copy-start(f32[3072]{0:T(1024)} %param.33) | copy-start | bytes 36868
  88.2 14.6 %slice-start.3 = ((s8[4718592]{0:T(1024)(128)(4,1)}), s8[4194304]{0:T(1024)(128)(4,1)S(1)}, s32[]{:S(2)}) async-start(s8[4718592]{0:T(1024)(128)(4,1)} %bitcast.125), calls=%async_computation.12 | async-start | bytes 8388608
  93.9 8.8 %copy-start.45 = (f32[512,3072]{1,0:T(8,128)}, f32[512,3072]{1,0:T(8,128)S(1)}, u32[]{:S(2)}) copy-start(f32[512,3072]{1,0:T(8,128)S(1)} %fusion.59) | copy-start | bytes 18874372
  94.0 8.8 %slice-start.4 = ((s8[4718592]{0:T(1024)(128)(4,1)}), s8[524288]{0:T(1024)(128)(4,1)S(1)}, s32[]{:S(2)}) async-start(s8[4718592]{0:T(1024)(128)(4,1)} %bitcast.125), calls=%async_computation.13 | async-start | bytes 1048576
  102.7 3.5 copy-start.46
  107.0 1.1 copy-start.2
  107.0 5.2 copy-start.27
  109.1 0.9 copy-start.14
  112.3 118.7 %reduce-scatter.5.cloned.1.call-start = ((), (), s32[]{:S(2)}) async-start(), calls=%async_computation.4 | async-start | bytes 7962624 | tf_op jit(solution)/shard_map/reduce_scatter | solution.py:218
  112.3 3.2 copy-start.20
  112.3 3.2 copy-start.23
  118.5 13.5 %slice-start = ((s8[12582912]{0:T(1024)(128)(4,1)}), s8[4194304]{0:T(1024)(128)(4,1)S(1)}, s32[]{:S(2)}) async-start(s8[12582912]{0:T(1024)(128)(4,1)} %bitcast.105), calls=%async_computation.9 | async-start | bytes 8388608
  118.5 13.5 %slice-start.1 = ((s8[12582912]{0:T(1024)(128)(4,1)}), s8[4194304]{0:T(1024)(128)(4,1)S(1)}, s32[]{:S(2)}) async-start(s8[12582912]{0:T(1024)(128)(4,1)} %bitcast.105), calls=%async_computation.10 | async-start | bytes 8388608
  118.5 13.5 %slice-start.2 = ((s8[12582912]{0:T(1024)(128)(4,1)}), s8[4194304]{0:T(1024)(128)(4,1)S(1)}, s32[]{:S(2)}) async-start(s8[12582912]{0:T(1024)(128)(4,1)} %bitcast.105), calls=%async_computation.11 | async-start | bytes 8388608
  118.5 13.5 %copy-start.8 = (pred[512,512]{0,1:T(8,128)(4,1)S(1)}, pred[512,512]{0,1:T(8,128)(4,1)}, u32[]{:S(2)}) copy-start(pred[512,512]{0,1:T(8,128)(4,1)} %fusion.36) | copy-start | bytes 786436
  118.5 13.5 %copy-start.21 = (f32[12,512]{1,0:T(8,128)S(1)}, f32[12,512]{1,0:T(8,128)}, u32[]{:S(2)}) copy-start(f32[12,512]{1,0:T(8,128)} %log_add_fusion) | copy-start | bytes 73732
  132.0 7.3 %copy-start.7 = (bf16[512,768]{0,1:T(8,128)(2,1)S(1)}, bf16[512,768]{0,1:T(8,128)(2,1)}, u32[]{:S(2)}) copy-start(bf16[512,768]{0,1:T(8,128)(2,1)} %copy.54) | copy-start | bytes 2359300
  139.4 2.9 copy-start.6
  142.3 1.2 copy-start.12
  143.5 4.0 copy-start.15
  143.5 4.9 copy-start.4
  143.5 4.9 copy-start.18
  143.5 4.9 copy-start.25
  143.5 4.9 copy-start.31
  143.5 4.9 copy-start.41
  147.5 0.9 copy-start.44
  153.7 177.5 %reduce-scatter.11.cloned.1.call-start = ((), (), s32[]{:S(2)}) async-start(), calls=%async_computation.7 | async-start | bytes 10616832 | tf_op jit(solution)/shard_map/reduce_scatter | solution.py:229
  163.9 267.3 %reduce-scatter.9.cloned.1.call-start = ((), (), s32[]{:S(2)}) async-start(), calls=%async_computation.6 | async-start | bytes 10616832 | tf_op jit(solution)/shard_map/reduce_scatter | solution.py:227
  173.2 354.1 %all-reduce.14.cloned.1.call-start = ((), (), s32[]{:S(2)}) async-start(), calls=%async_computation.8 | async-start | bytes 7077888 | tf_op jit(solution)/shard_map/psum | solution.py:232
  435.8 4.9 copy-start.30
  435.8 4.9 copy-start.5
  435.8 4.9 copy-start.26
  435.8 4.9 copy-start.32
  440.7 1.5 copy-start.11
  492.6 3.8 copy-start.10
  492.6 3.8 copy-start.39
  492.6 3.8 copy-start.43
  527.3 4.0 copy-start.17
  527.3 5.0 copy-start.16
Sparse Core Ops, SparseCore 0:
  112.4 36.3 reduce-scatter.6
  153.8 77.1 reduce-scatter.4
  233.3 97.8 reduce-scatter.10
  333.4 97.8 reduce-scatter.8
  434.6 92.6 all-reduce.13
where the time goes:
time: 550 us; the launch traced here: 540 us
  waiting for transfers between devices  280 us (51%)
  matrix products  95.8 us (17%)
  blocking collectives  80.4 us (15%)
  local copies, waits for them, and re-layouts  35.4 us (6%)
  other arithmetic  28 us (5%)
  between operations  20.3 us (4%)
    reduce_scatter x1, waiting for transfers between devices, shards(): lax.psum_scatter(down_weight_grad, 'dp', scatter_dimension=0, tiled=True)  100 us
    reduce_scatter x1, waiting for transfers between devices, shards(): lax.psum_scatter(up_weight_grad, 'dp', scatter_dimension=0, tiled=True)  100 us
    reduce_scatter x1, waiting for transfers between devices, shards(): lax.psum_scatter(proj_weight_grad, 'dp', scatter_dimension=0, tiled=True)  57.7 us
    psum x1, blocking collectives, shards(): totals = lax.psum(count_terms, ('group', 'dp'))  42 us
    unnamed x1, blocking collectives  27.5 us
    dot_general x4, matrix products, outer_product(): lax.dot_general(left, right, (((0,), (0,)), ((), ())), preferred_element_...  26.6 us
    unnamed x122, local copies, waits for them, and re-layouts  22.6 us
    psum x1, waiting for transfers between devices, shards(): summed = lax.psum(tuple(shares), 'group')  21.9 us
  transfers between devices with their start and end apart: 5, of which 4 were waited for; matrix products, arithmetic and copies ran while one was open for 17% of the time, Pallas kernels for 0%

commit v1 on v0

--- a/solution.py
+++ b/solution.py
@@ -1,9 +1,17 @@
+import functools
+import math
+
 import jax
 import jax.numpy as jnp
 from jax import lax
+from jax.experimental import pallas as pl
+from jax.experimental.pallas import tpu as pltpu
 from jax.sharding import PartitionSpec as P
 
 HEAD_DIM = 64
+LANES = 128
+SUBLANES = 8
+MESH = pl.DeviceIdType.MESH
 
 
 eps_norm = 1e-05
@@ -112,7 +120,7 @@
     return (query_grad.reshape(query_heads.shape), key_grad, value_grad)
 
 
-def shards(
+def plain_shards(
     tokens,
     cotangent,
     replay_count,
@@ -234,6 +242,773 @@
     return (output, tokens_grad) + pieces
 
 
+def bit_of(number, place):
+    return lax.rem(lax.div(number, 2**place), 2)
+
+
+def flip(number, place):
+    return number + (1 - 2 * bit_of(number, place)) * 2**place
+
+
+class Places:
+    def __init__(self, group_bits, dp_bits):
+        group, spot = lax.axis_index("group"), lax.axis_index("dp")
+        core = lax.rem(spot, 2)
+        half = group_bits // 2
+
+        def pick(place):
+            one, two = (place + half) % group_bits, place % group_bits
+            flipped = flip(group, one) + core * (flip(group, two) - flip(group, one))
+            side = bit_of(group, one) + core * (bit_of(group, two) - bit_of(group, one))
+            return (flipped, spot), side
+
+        self.core = core
+        self.partners = [(group, flip(spot, 0))]
+        self.sides = [core]
+        first, side = pick(0)
+        self.partners.append(first)
+        self.sides.append(side)
+        for place in range(1, dp_bits):
+            self.partners.append((group, flip(spot, place)))
+            self.sides.append(bit_of(spot, place))
+        for place in range(1, group_bits):
+            other, side = pick(place)
+            self.partners.append(other)
+            self.sides.append(side)
+
+
+class Ring:
+    def __init__(self, group_bits, dp_bits, chunks, tiles):
+        self.group_bits, self.dp_bits, self.chunks, self.tiles = group_bits, dp_bits, chunks, tiles
+        self.blocks = 2 ** (dp_bits - 1)
+        self.z_stages = dp_bits - 1
+        self.b_stages = group_bits - 1
+        self.stages = 2 + self.z_stages + self.b_stages + 1
+        self.lags = (2,) * self.stages
+        self.after = [0, 0]
+        for lag in self.lags[1:-1]:
+            self.after.append(self.after[-1] + lag)
+        self.order = tuple(range(self.stages - 1, 1, -1))
+        self.steps = chunks + self.after[-1]
+
+    def scratch(self):
+        half, blocks, lags = self.tiles // 2, self.blocks, self.lags
+        tile = (half, SUBLANES, LANES)
+        shapes = [(blocks, 2, 2) + tile, (blocks, 2) + tile]
+        landing = [(blocks, 2) + tile, (blocks,) + tile]
+        left = blocks
+        for _ in range(self.z_stages):
+            left //= 2
+            shapes.append((left, 2) + tile)
+            landing.append((left,) + tile)
+        shapes += [tile] * self.b_stages
+        landing += [tile] * self.b_stages
+        send = [pltpu.VMEM((lag,) + shape, jnp.float32) for lag, shape in zip(lags, shapes)]
+        recv = [pltpu.VMEM((2 * lag,) + shape, jnp.float32) for lag, shape in zip(lags, landing)]
+        send_sems = [pltpu.SemaphoreType.DMA((lag,)) for lag in lags]
+        recv_sems = [pltpu.SemaphoreType.DMA((2 * lag,)) for lag in lags]
+        return [send, recv, send_sems, recv_sems]
+
+    def bind(self, places, scratch, final):
+        self.places = places
+        self.send, self.recv, self.send_sems, self.recv_sems = scratch
+        self.final = final
+
+    def sending(self, stage, chunk):
+        return self.send[stage].at[lax.rem(chunk, self.lags[stage])]
+
+    def half_of(self, stage, ref, side):
+        return ref.at[:, side] if stage < 2 + self.z_stages else ref
+
+    def remote(self, source, goal, send_sem, recv_sem, target):
+        return pltpu.make_async_remote_copy(
+            src_ref=source,
+            dst_ref=goal,
+            send_sem=send_sem,
+            recv_sem=recv_sem,
+            device_id=target,
+            device_id_type=MESH,
+        )
+
+    def copy(self, stage, chunk):
+        lag, places = self.lags[stage], self.places
+        send_sem = self.send_sems[stage].at[lax.rem(chunk, lag)]
+        recv_sem = self.recv_sems[stage].at[lax.rem(chunk, 2 * lag)]
+        source = self.half_of(stage, self.sending(stage, chunk), 1 - places.sides[stage])
+        goal = self.recv[stage].at[lax.rem(chunk, 2 * lag)]
+        return self.remote(source, goal, send_sem, recv_sem, places.partners[stage])
+
+    def gather(self, part):
+        half = self.final.at[part, self.places.sides[1]]
+        last = self.stages - 1
+        return self.remote(half, half, self.send_sems[last].at[0], self.recv_sems[last].at[0], self.places.partners[1])
+
+    def gathered(self):
+        return self.gather(slice(None))
+
+    def advance(self, stage, chunk):
+        past = stage - 1
+        before = self.copy(past, chunk)
+        before.wait_recv()
+        mine = self.half_of(past, self.sending(past, chunk), self.places.sides[past])
+        theirs = self.recv[past].at[lax.rem(chunk, 2 * self.lags[past])]
+        last = stage == self.stages - 1
+        goal = self.final.at[chunk, self.places.sides[1]] if last else self.sending(stage, chunk)
+        goal[...] = (mine[...] + theirs[...]).reshape(goal.shape)
+        (self.gather(chunk) if last else self.copy(stage, chunk)).start()
+        before.wait_send()
+
+    def pump(self, step, full):
+        for stage in self.order:
+            chunk = step - self.after[stage]
+            if full:
+                self.advance(stage, chunk)
+                continue
+
+            @pl.when((chunk >= 0) & (chunk < self.chunks))
+            def _():
+                self.advance(stage, chunk)
+
+
+def contract_rows(left, right):
+    return lax.dot_general(left, right, (((0,), (0,)), ((), ())), preferred_element_type=jnp.float32)
+
+
+SLAB = 512
+PAIR = 2 * HEAD_DIM
+ROWS_AT_ONCE = 128
+NARROW = ("query", "value", "out", "gain1", "shift1", "gain2", "shift2", "down")
+
+
+def slab(index, width):
+    return pl.ds(pl.multiple_of(index * width, width), width)
+
+
+def moments(rows):
+    centered = rows - jnp.mean(rows, axis=-1, keepdims=True)
+    variance = jnp.mean(centered * centered, axis=-1, keepdims=True)
+    return centered, lax.rsqrt(variance + eps_norm)
+
+
+def gelu_and_slope(inputs):
+    root = math.sqrt(2.0 / math.pi)
+    square = inputs * inputs
+    bent = jnp.tanh(root * (inputs + 0.044715 * (square * inputs)))
+    rise = 0.5 + 0.5 * bent
+    slope = rise + (0.5 * root) * inputs * (1.0 - bent * bent) * (1.0 + 3 * 0.044715 * square)
+    return inputs * rise, slope
+
+
+def norm_back(grad_rows, centered, rstd, gain):
+    hat = centered * rstd
+    gained = grad_rows * gain
+    inner = jnp.mean(gained * hat, axis=-1, keepdims=True)
+    back = (gained - jnp.mean(gained, axis=-1, keepdims=True) - hat * inner) * rstd
+    sums = (jnp.sum(grad_rows * hat, axis=0, keepdims=True), jnp.sum(grad_rows, axis=0, keepdims=True))
+    return back, sums
+
+
+def layer_kernel(ring, slots, dp_size, *refs):
+    (
+        tokens_ref, cotangent_hbm, replay_ref, length_ref, mask_ref, proj_hbm, query_bias_ref, value_bias_ref, out_hbm,
+        out_bias_ref, gain1_ref, shift1_ref, gain2_ref, shift2_ref, up_hbm, up_bias_ref, down_hbm, down_bias_ref,
+        low_ref, grad_ref, final_ref, bias_ref,
+        proj_ref, out_ref, up_ref, down_ref, norm1_ref, heads_ref, mixed_ref, residual_ref, norm2_ref, act_ref,
+        hidden_ref, branch_ref, weight_ref, sum_ref, attn_ref, mixed_grad_ref, heads_grad_ref, log_ref,
+        mixed_turned_ref, turned_ref, pad_ref, key_sum_ref, value_sum_ref, cotangent_ref, load_sems, small_send, small_recv, small_sems, wide_send, wide_recv, wide_sems, *scratch
+    ) = refs
+    f32, bf16 = jnp.float32, jnp.bfloat16
+    token_count, width = tokens_ref.shape
+    half_scale = HEAD_DIM ** (-0.5)
+    places = Places(ring.group_bits, ring.dp_bits)
+    turns = len(places.partners)
+    stages = ring.stages
+    sems = scratch[2 * stages - 2 :]
+    ring.bind(
+        places,
+        (scratch[: stages - 1], scratch[stages - 1 : 2 * stages - 2], sems[:stages], sems[stages:]),
+        final_ref,
+    )
+
+    loads = [
+        pltpu.make_async_copy(source, goal, load_sems.at[place])
+        for place, (source, goal) in enumerate(
+            (
+                (proj_hbm, proj_ref),
+                (out_hbm, out_ref),
+                (up_hbm, up_ref),
+                (down_hbm, down_ref),
+                (cotangent_hbm, cotangent_ref),
+            )
+        )
+    ]
+    for load in loads:
+        load.start()
+
+    barrier = pltpu.get_barrier_semaphore()
+    for partner in places.partners:
+        pl.semaphore_signal(barrier, inc=1, device_id=partner, device_id_type=MESH)
+
+    def exchange(buffers, landing, sems, turn):
+        return pltpu.make_async_remote_copy(
+            src_ref=buffers.at[turn],
+            dst_ref=landing.at[turn],
+            send_sem=sems.at[0, turn],
+            recv_sem=sems.at[1, turn],
+            device_id=places.partners[turn],
+            device_id_type=MESH,
+        )
+
+    small = functools.partial(exchange, small_send, small_recv, small_sems)
+    wide = functools.partial(exchange, wide_send, wide_recv, wide_sems)
+
+    group_half = 2**ring.group_bits // 2
+    group = lax.axis_index("group")
+    row = group * dp_size + lax.axis_index("dp")
+    row_blocks = [slice(at, at + ROWS_AT_ONCE) for at in range(0, token_count, ROWS_AT_ONCE)]
+    for rows in row_blocks:
+        centered, rstd = moments(tokens_ref[rows, :].astype(f32))
+        norm1_ref[rows, :] = (centered * rstd * gain1_ref[...] + shift1_ref[...]).astype(bf16)
+
+    used = jnp.where((group >= group_half) | (row < replay_ref[0]), 1.0, 0.0)
+    live = mask_ref[...].astype(f32) * used
+    side = lax.div(group, group_half)
+    tile_rows = lax.broadcasted_iota(jnp.int32, (SUBLANES, LANES), 0)
+    small_send[0] = jnp.where(tile_rows == side, jnp.sum(live, axis=1, keepdims=True), 0.0)
+    loads[0].wait()
+    for third, bias in enumerate((query_bias_ref, None, value_bias_ref)):
+
+        columns = slice(third * width, (third + 1) * width)
+        product = plain_product(norm1_ref[...], proj_ref[:, columns])
+        if bias is not None:
+            product = product + bias[...]
+        heads_ref[:, columns] = product.astype(bf16)
+
+    pl.semaphore_wait(barrier, turns)
+
+    length = length_ref[0]
+    lanes = lax.broadcasted_iota(jnp.int32, (1, PAIR), 1)
+    own_lanes = (lanes < HEAD_DIM, lanes >= HEAD_DIM)
+    spare_lanes = (lanes == HEAD_DIM, lanes == 0)
+    block = token_count // 2
+    blocks = ((0, block), (block, token_count))
+    causal = lax.broadcasted_iota(jnp.int32, (block, block), 0) <= lax.broadcasted_iota(jnp.int32, (block, block), 1)
+    padding = lax.broadcasted_iota(jnp.int32, (token_count, PAIR), 0) >= length
+    for head in range(2):
+        pad_ref[head] = jnp.where(padding & spare_lanes[head], masked_score, 0.0).astype(bf16)
+
+    def pair_columns(third, pair):
+        return pl.ds(pl.multiple_of(third * width + pair * PAIR, PAIR), PAIR)
+
+    def only(head, array):
+        return jnp.where(own_lanes[head], array, jnp.zeros_like(array))
+
+    def head_scores(head, key, query, start, keys):
+        padded = jnp.where(own_lanes[head], key[:keys], pad_ref[head, :keys])
+        one = jnp.where(spare_lanes[head], 1.0, 0.0).astype(bf16)
+        asking = jnp.where(own_lanes[head], query[start : start + block] * half_scale, one)
+        scores = transposed_product(padded, asking)
+        last = jnp.where(causal, scores[start:], masked_score)
+        return last if start == 0 else jnp.concatenate([scores[:start], last], axis=0)
+
+    def attend(pair):
+        query = heads_ref[:, pair_columns(0, pair)]
+        key = heads_ref[:, pair_columns(1, pair)]
+        turned = heads_ref[:, pair_columns(2, pair)].T
+        for start, keys in blocks:
+            mixed = []
+            for head in range(2):
+                scores = head_scores(head, key, query, start, keys)
+                highest = jnp.max(scores, axis=0, keepdims=True)
+                raised = jnp.exp(scores - highest)
+                total = jnp.sum(raised, axis=0, keepdims=True)
+                log_ref[pair, head : head + 1, start : start + block] = highest + jnp.log(total)
+                product = plain_product(turned[head * HEAD_DIM : (head + 1) * HEAD_DIM, :keys], raised.astype(bf16))
+                mixed.append(product * (1.0 / total))
+            low = jnp.concatenate(mixed, axis=0).astype(bf16)
+            mixed_turned_ref[slab(pair, PAIR), start : start + block] = low
+            mixed_ref[start : start + block, slab(pair, PAIR)] = low.T
+
+    def count_turn(turn):
+        if turn:
+            small(turn - 1).wait()
+            small_send[turn] = small_send[turn - 1] + small_recv[turn - 1]
+        if turn < turns:
+            small(turn).start()
+
+    count_turn(0)
+
+    @pl.loop(0, width // (2 * PAIR))
+    def _(at):
+        attend(2 * at)
+        attend(2 * at + 1)
+        for turn in range(1, 4):
+
+            @pl.when(at + 1 == turn)
+            def _():
+                count_turn(turn)
+
+
+    loads[1].wait()
+
+    product = plain_product(mixed_ref[...], out_ref[...]) + out_bias_ref[...]
+    residual_ref[...] = tokens_ref[...].astype(f32) + product
+    count_turn(4)
+
+    for rows in row_blocks:
+        centered, rstd = moments(residual_ref[rows, :])
+        low = (centered * rstd * gain2_ref[...] + shift2_ref[...]).astype(bf16)
+        norm2_ref[rows, :] = low
+        turned_ref[:, rows] = low.T
+
+    for turn in range(5, turns + 1):
+        count_turn(turn)
+    loads[4].wait()
+
+    totals = jnp.sum(jnp.where(tile_rows == side, small_send[turns], 0.0), axis=0, keepdims=True)
+    weight_ref[...] = jnp.broadcast_to(live, (LANES, token_count)).T * (slots / totals)
+
+    def out_grad(rows):
+        pieces = [
+            cotangent_ref[rows, at * LANES : (at + 1) * LANES].astype(f32) * weight_ref[rows, :]
+            for at in range(width // LANES)
+        ]
+        return jnp.concatenate(pieces, axis=1)
+
+    def keep_narrow(name, vector):
+        place = NARROW.index(name)
+        for at in range(width // LANES):
+            wide_send[0, at * SUBLANES + place : at * SUBLANES + place + 1, :] = vector[:, at * LANES : (at + 1) * LANES]
+
+    def row_sums(body, count):
+        zeros = tuple(jnp.zeros((1, width), f32) for _ in range(count))
+
+        def one(at, sums):
+            return tuple(old + new for old, new in zip(sums, body(slab(at, ROWS_AT_ONCE))))
+
+        return lax.fori_loop(0, token_count // ROWS_AT_ONCE, one, zeros)
+
+    def branch_rows(rows):
+        low = out_grad(rows).astype(bf16)
+        branch_ref[rows, :] = low
+        return jnp.sum(low.astype(f32), axis=0, keepdims=True)
+
+    keep_narrow("down", sum(branch_rows(rows) for rows in row_blocks))
+
+    goal = ring.send[0]
+    halves, blocks_of = ring.tiles // 2, ring.blocks
+
+    def put(column, product):
+        rows = product.shape[0] // (2 * blocks_of * SUBLANES)
+        shaped = product.reshape(blocks_of, 2, rows, SUBLANES, LANES)
+        for part in range(rows // halves):
+            place = column * (rows // halves) + part
+            goal[place // 2, :, :, place % 2] = shaped[:, :, part * halves : (part + 1) * halves]
+
+    def put_all(product):
+        for column in range(SLAB // LANES):
+            put(column, product[:, column * LANES : (column + 1) * LANES])
+
+    def one_step(step, make, work, more, full=True):
+        first = 2 * step
+        make()
+        ring.copy(0, first).start()
+        ring.copy(0, first + 1).start()
+        work()
+        ring.pump(first, full)
+        ring.advance(1, first)
+        more()
+        ring.pump(first + 1, full)
+        ring.advance(1, first + 1)
+
+    loads[2].wait()
+    loads[3].wait()
+    slabs = up_ref.shape[1] // SLAB
+    narrow_rows = width // LANES * SUBLANES
+
+    def hidden_slab(at, size=SLAB):
+        columns = slab(at, size)
+        hidden = plain_product(norm2_ref[...], up_ref[:, columns]) + up_bias_ref[columns]
+        act, slope = gelu_and_slope(hidden)
+        act_ref[columns, :] = act.astype(bf16).T
+        low = (transposed_product(branch_ref[...], down_ref[columns, :]) * slope).astype(bf16)
+        hidden_ref[:, columns] = low
+        bias_sum = jnp.sum(low.astype(f32), axis=0, keepdims=True)
+        for part in range(size // LANES):
+            place = narrow_rows + at * (size // LANES) + part
+            wide_send[0, pl.ds(place, 1), :] = bias_sum[:, part * LANES : (part + 1) * LANES]
+
+    for part in range(2):
+        hidden_slab(part, SLAB // 2)
+        columns = slice(part * SLAB // 2, (part + 1) * SLAB // 2)
+        product = plain_product(turned_ref[...], hidden_ref[:, columns])
+        for column in range(2):
+            put(2 * part + column, product[:, column * LANES : (column + 1) * LANES])
+        ring.copy(0, part).start()
+    ring.advance(1, 0)
+    grad_ref[...] = transposed_product(hidden_ref[:, :SLAB], up_ref[:, :SLAB])
+    ring.advance(1, 1)
+    hidden_slab(1)
+
+    @pl.loop(1, slabs)
+    def _(step):
+        columns = slab(step, SLAB)
+
+        def make():
+            put_all(plain_product(turned_ref[...], hidden_ref[:, columns]))
+
+        def work():
+            @pl.when(step + 1 < slabs)
+            def _():
+                hidden_slab(step + 1)
+
+        def more():
+            grad_ref[...] += transposed_product(hidden_ref[:, columns], up_ref[:, columns])
+
+        one_step(step, make, work, more, full=False)
+
+    def second_back(rows):
+        residual = residual_ref[rows, :]
+        turned_ref[:, rows] = norm1_ref[rows, :].T
+        centered, rstd = moments(residual)
+        back, sums = norm_back(grad_ref[rows, :], centered, rstd, gain2_ref[...])
+        residual_grad = out_grad(rows) + back
+        grad_ref[rows, :] = residual_grad
+        low = residual_grad.astype(bf16)
+        attn_ref[rows, :] = low
+        return sums + (jnp.sum(low.astype(f32), axis=0, keepdims=True),)
+
+    def pair_back(pair, part):
+        start, keys = blocks[part]
+        here = slice(start, start + block)
+        query = heads_ref[:, pair_columns(0, pair)]
+        key = heads_ref[:, pair_columns(1, pair)]
+        value = heads_ref[:, pair_columns(2, pair)]
+        grad = mixed_grad_ref[here, slab(pair, PAIR)]
+        key_turned = key[:keys].T
+        query_grads, key_grad, value_grad = [], 0.0, 0.0
+        for head in range(2):
+            scores = head_scores(head, key, query, start, keys)
+            probs = jnp.exp(scores - log_ref[pair, head : head + 1, here])
+            value_grad += plain_product(probs.astype(bf16), only(head, grad))
+            prob_grad = transposed_product(only(head, value[:keys]), grad)
+            inner = jnp.sum(prob_grad * probs, axis=0, keepdims=True)
+            low = (probs * (prob_grad - inner)).astype(bf16)
+            query_grads.append(plain_product(key_turned[head * HEAD_DIM : (head + 1) * HEAD_DIM], low))
+            key_grad += plain_product(low, only(head, query[here]))
+        query_low = (jnp.concatenate(query_grads, axis=0) * half_scale).astype(bf16).T
+        heads_grad_ref[here, pair_columns(0, pair)] = query_low
+        keep_pair("query", pair, part, query_low)
+        if part == 0:
+            key_sum_ref[...] = key_grad
+            value_sum_ref[...] = value_grad
+            return
+        for third, total, factor, earlier in (
+            (1, key_grad, half_scale, key_sum_ref),
+            (2, value_grad, 1.0, value_sum_ref),
+        ):
+            first = ((total[:block] + earlier[...]) * factor).astype(bf16)
+            second = (total[block:] * factor).astype(bf16)
+            heads_grad_ref[:block, pair_columns(third, pair)] = first
+            heads_grad_ref[block:, pair_columns(third, pair)] = second
+            if third == 2:
+                keep_pair("value", pair, 0, first)
+                keep_pair("value", pair, 1, second)
+
+    def keep_pair(name, pair, part, low):
+        place = pl.ds(pair * SUBLANES + NARROW.index(name), 1)
+        total = jnp.sum(low.astype(f32), axis=0, keepdims=True)
+        wide_send[0, place, :] = total + wide_send[0, place, :] if part else total
+
+    def make_down(step):
+        pair, part = lax.div(step - slabs, 2), lax.rem(step - slabs, 2)
+        rows = act_ref.shape[0] // (2 * blocks_of)
+        starts = [pl.multiple_of(place * rows + part * (rows // 2), 2 * SUBLANES) for place in range(2 * blocks_of)]
+        tall = jnp.concatenate([act_ref[pl.ds(start, rows // 2), :] for start in starts], axis=0)
+        product = plain_product(tall, branch_ref[:, slab(pair, 2 * LANES)])
+        for column in range(2):
+            put(column, product[:, column * LANES : (column + 1) * LANES])
+
+    def second_norm():
+        for name, vector in zip(("gain2", "shift2", "out"), row_sums(second_back, 3)):
+            keep_narrow(name, vector)
+
+    def mixed_back():
+        mixed_grad_ref[...] = transposed_product(attn_ref[...], out_ref[...]).astype(bf16)
+
+    one_step(slabs, functools.partial(make_down, slabs), second_norm, mixed_back)
+
+    @pl.loop(slabs + 1, 2 * slabs)
+    def _(step):
+        pair = step - slabs - 1
+        one_step(
+            step,
+            functools.partial(make_down, step),
+            functools.partial(pair_back, pair, 0),
+            functools.partial(pair_back, pair, 1),
+        )
+
+    def make_out():
+        put_all(plain_product(mixed_turned_ref[...], attn_ref[:, :SLAB]))
+
+    step = 2 * slabs
+    pair = slabs - 1
+    one_step(step, make_out, functools.partial(pair_back, pair, 0), functools.partial(pair_back, pair, 1))
+
+    rest = width - SLAB
+
+    def make_both():
+        part = plain_product(mixed_turned_ref[...], attn_ref[:, SLAB:])
+        more = plain_product(turned_ref[...], heads_grad_ref[:, : SLAB - rest])
+        for column in range(rest // LANES):
+            put(column, part[:, column * LANES : (column + 1) * LANES])
+        for column in range((SLAB - rest) // LANES):
+            put(column + rest // LANES, more[:, column * LANES : (column + 1) * LANES])
+
+    def norm1_grads():
+        sum_ref[...] = transposed_product(heads_grad_ref[...], proj_ref[...])
+
+    def first_back(rows):
+        centered, rstd = moments(tokens_ref[rows, :].astype(f32))
+        back, sums = norm_back(sum_ref[rows, :], centered, rstd, gain1_ref[...])
+        grad_ref[rows, :] += back
+        return sums
+
+    def first_norm():
+        for name, vector in zip(("gain1", "shift1"), row_sums(first_back, 2)):
+            keep_narrow(name, vector)
+        wide(0).start()
+
+    step += 1
+    one_step(step, make_both, norm1_grads, first_norm)
+    step += 1
+
+    def add_branch(at):
+        columns = slab(at, SLAB)
+        residual_ref[...] += contract_rows(act_ref[columns, :], down_ref[columns, :])
+
+    def wide_turn(now, first):
+        for turn in range(turns):
+
+            @pl.when(now == first + turn)
+            def _():
+                wide(turn).wait()
+                wide_send[turn + 1] = wide_send[turn] + wide_recv[turn]
+                if turn + 1 < turns:
+                    wide(turn + 1).start()
+
+    last_steps = 3 * slabs - step
+
+    @pl.loop(step, 3 * slabs)
+    def _(now):
+        def make():
+            start = pl.multiple_of((now - step) * SLAB + SLAB - rest, LANES)
+            put_all(plain_product(turned_ref[...], heads_grad_ref[:, pl.ds(start, SLAB)]))
+
+        def work():
+            wide_turn(now, step)
+
+            @pl.when(now - step < slabs // 2)
+            def _():
+                add_branch(now - step)
+
+        def more():
+            @pl.when(now - step < slabs // 2)
+            def _():
+                add_branch(now - step + slabs // 2)
+
+        one_step(now, make, work, more)
+
+    @pl.loop(ring.chunks, ring.steps)
+    def _(now):
+        ring.pump(now, False)
+        wide_turn(now, ring.chunks - last_steps)
+
+        @pl.when(now == ring.chunks)
+        def _():
+            low_ref[...] = (residual_ref[...] + down_bias_ref[...]).astype(bf16)
+
+    ring.gathered().wait()
+    bias_ref[...] = wide_send[turns]
+
+
+def layer(group_size, dp_size, slots, arrays):
+    f32, bf16 = jnp.float32, jnp.bfloat16
+    group_bits, dp_bits = int(math.log2(group_size)), int(math.log2(dp_size))
+    token_count, width = arrays[0].shape
+    hidden = arrays[14].shape[1]
+    ring = Ring(group_bits, dp_bits, 6 * hidden // SLAB, hidden // dp_size // SUBLANES // 2)
+    turns = group_bits + dp_bits
+    send, recv, send_sems, recv_sems = ring.scratch()
+    tile = (SUBLANES, LANES)
+    wide = ((len(NARROW) * width + hidden) // LANES, LANES)
+    vmem, anywhere = pl.BlockSpec(memory_space=pltpu.VMEM), pl.BlockSpec(memory_space=pl.ANY)
+    in_specs = [vmem] * len(arrays)
+    for place in (1, 5, 8, 14, 16):
+        in_specs[place] = anywhere
+    for place in (2, 3):
+        in_specs[place] = pl.BlockSpec(memory_space=pltpu.SMEM)
+    return pl.pallas_call(
+        functools.partial(layer_kernel, ring, slots, dp_size),
+        out_shape=(
+            pltpu.VMEM((token_count, width), bf16),
+            pltpu.VMEM((token_count, width), f32),
+            pltpu.VMEM((ring.chunks, 2, ring.tiles // 2) + tile, f32),
+            pltpu.VMEM(wide, f32),
+        ),
+        in_specs=in_specs,
+        out_specs=(vmem,) * 4,
+        scratch_shapes=[
+            pltpu.VMEM((width, 3 * width), bf16),
+            pltpu.VMEM((width, width), bf16),
+            pltpu.VMEM((width, hidden), bf16),
+            pltpu.VMEM((hidden, width), bf16),
+            pltpu.VMEM((token_count, width), bf16),
+            pltpu.VMEM((token_count, 3 * width), bf16),
+            pltpu.VMEM((token_count, width), bf16),
+            pltpu.VMEM((token_count, width), f32),
+            pltpu.VMEM((token_count, width), bf16),
+            pltpu.VMEM((hidden, token_count), bf16),
+            pltpu.VMEM((token_count, hidden), bf16),
+            pltpu.VMEM((token_count, width), bf16),
+            pltpu.VMEM((token_count, LANES), f32),
+            pltpu.VMEM((token_count, width), f32),
+            pltpu.VMEM((token_count, width), bf16),
+            pltpu.VMEM((token_count, width), bf16),
+            pltpu.VMEM((token_count, 3 * width), bf16),
+            pltpu.VMEM((width // PAIR, 2, token_count), f32),
+            pltpu.VMEM((width, token_count), bf16),
+            pltpu.VMEM((width, token_count), bf16),
+            pltpu.VMEM((2, token_count, PAIR), bf16),
+            pltpu.VMEM((token_count // 2, PAIR), f32),
+            pltpu.VMEM((token_count // 2, PAIR), f32),
+            pltpu.VMEM((token_count, width), bf16),
+            pltpu.SemaphoreType.DMA((5,)),
+            pltpu.VMEM((turns + 1,) + tile, f32),
+            pltpu.VMEM((turns,) + tile, f32),
+            pltpu.SemaphoreType.DMA((2, turns)),
+            pltpu.VMEM((turns + 1,) + wide, f32),
+            pltpu.VMEM((turns,) + wide, f32),
+            pltpu.SemaphoreType.DMA((2, turns)),
+        ]
+        + send
+        + recv
+        + send_sems
+        + recv_sems,
+        compiler_params=pltpu.CompilerParams(
+            collective_id=0, has_side_effects=True, vmem_limit_bytes=54 * 2**20
+        ),
+    )(*arrays)
+
+
+def place_kernel(*refs):
+    low_ref, grad_ref, tiles_ref, bias_ref = refs[:4]
+    goals = refs[4:19]
+    proj_ref, out_ref, up_ref, down_ref = refs[19:23]
+    narrow_refs, up_bias_ref, store_sems = refs[23:31], refs[31], refs[32]
+    chunks, _, half = tiles_ref.shape[:3]
+    third = chunks // 3
+    sources = (low_ref, grad_ref, proj_ref, out_ref, up_ref, down_ref) + narrow_refs + (up_bias_ref,)
+    stores = [pltpu.make_async_copy(*pair, store_sems.at[place]) for place, pair in enumerate(zip(sources, goals))]
+    for store in stores[:2]:
+        store.start()
+    rows = proj_ref.shape[0]
+    width = out_ref.shape[2]
+    out_columns = width // LANES
+    spot = lax.axis_index("dp")
+    piece = rows * SUBLANES
+    columns = width // LANES
+    vectors = jnp.concatenate(
+        [bias_ref[at * SUBLANES : (at + 1) * SUBLANES, :] for at in range(columns)], axis=1
+    )
+    vectors = pltpu.roll(vectors, lax.rem(width - spot * piece, width), 1)
+    for place, ref in enumerate(narrow_refs):
+        ref[...] = vectors[place, :piece]
+    count = up_bias_ref.shape[0] // LANES
+    for at in range(count):
+        row = columns * SUBLANES + spot * count + at
+        up_bias_ref[at * LANES : (at + 1) * LANES] = bias_ref[pl.ds(row, 1), :].reshape(LANES)
+    for store in stores[6:]:
+        store.start()
+    parts = down_ref.shape[0] // half
+    for place in range(2 * third):
+        pair, inside = divmod(place, 2 * parts)
+        part, column = divmod(inside, parts)
+        part, column = 2 * part + column % 2, 2 * pair + column // 2
+        goal = down_ref.at[part * half : (part + 1) * half, :, column * LANES : (column + 1) * LANES]
+        goal[...] = tiles_ref[third + place // 2, place % 2]
+    stores[5].start()
+    for kind in (0, 2):
+        for column in range(third * 2 * (half // rows)):
+            place, part = divmod(column, half // rows)
+            goal, at = up_ref, column
+            if kind == 2:
+                goal, at = (out_ref, column) if column < out_columns else (proj_ref, column - out_columns)
+            source = tiles_ref[kind * third + place // 2, place % 2, part * rows : (part + 1) * rows]
+            goal[:, :, at * LANES : (at + 1) * LANES] = source
+        for store in stores[2:4] if kind else stores[4:5]:
+            store.start()
+    for store in stores:
+        store.wait()
+
+
+def place_results(dp_size, hidden, output, tokens_grad, final, bias):
+    f32 = jnp.float32
+    width = output.shape[1]
+    rows = width // dp_size
+    tile_rows = rows // SUBLANES
+    shape = jax.ShapeDtypeStruct
+    anywhere, vmem = pl.BlockSpec(memory_space=pl.ANY), pl.BlockSpec(memory_space=pltpu.VMEM)
+    large = (
+        (output.shape, output.dtype),
+        (tokens_grad.shape, f32),
+        ((tile_rows, SUBLANES, 3 * width), f32),
+        ((tile_rows, SUBLANES, width), f32),
+        ((tile_rows, SUBLANES, hidden), f32),
+        ((hidden // dp_size // SUBLANES, SUBLANES, width), f32),
+    )
+    vectors = (((rows,), f32),) * len(NARROW) + (((hidden // dp_size,), f32),)
+    return pl.pallas_call(
+        place_kernel,
+        out_shape=tuple(shape(*one) for one in large + vectors),
+        in_specs=[vmem] * 4,
+        out_specs=(anywhere,) * len(large + vectors),
+        scratch_shapes=[pltpu.VMEM(*one) for one in large[2:] + vectors]
+        + [pltpu.SemaphoreType.DMA((len(large + vectors),))],
+        compiler_params=pltpu.CompilerParams(vmem_limit_bytes=16 * 2**20),
+    )(output, tokens_grad, final, bias)
+
+
+def ring_shards(*arrays):
+    group_size, dp_size = lax.axis_size("group"), lax.axis_size("dp")
+    tokens = arrays[0]
+    _, token_count, width = tokens.shape
+    hidden = arrays[14].shape[1]
+    slots = float(dp_size * (group_size // 2) * token_count)
+    flat = [tokens[0], arrays[1][0], *arrays[2:]]
+    placed = place_results(dp_size, hidden, *layer(group_size, dp_size, slots, flat))
+    output, tokens_grad, proj, out, up, down = placed[:6]
+    narrow = dict(zip(NARROW, placed[6:14]))
+    rows = width // dp_size
+    return (
+        output[None],
+        tokens_grad[None],
+        proj.reshape(rows, 3 * width),
+        narrow["query"],
+        narrow["value"],
+        out.reshape(rows, width),
+        narrow["out"],
+        narrow["gain1"],
+        narrow["shift1"],
+        narrow["gain2"],
+        narrow["shift2"],
+        up.reshape(rows, hidden),
+        placed[14],
+        down.reshape(hidden // dp_size, width),
+        narrow["down"],
+    )
+
+
 def solution(mesh):
     in_specs = (
         P(("group", "dp"), None, None),
@@ -272,4 +1047,13 @@
         P("dp", None),
         P("dp"),
     )
-    return jax.shard_map(shards, mesh=mesh, in_specs=in_specs, out_specs=out_specs, check_vma=False)
+    group_size, dp_size = mesh.shape["group"], mesh.shape["dp"]
+
+    def body(*arrays):
+        tokens, out_weight, up_weight = arrays[0], arrays[8], arrays[14]
+        whole_tiles = (out_weight.shape[0] // dp_size) % SUBLANES == 0
+        one_row = tokens.shape[:2] == (1, 512) and up_weight.shape == (768, 3072)
+        powers = group_size == 4 and dp_size >= 4 and dp_size & (dp_size - 1) == 0
+        return (ring_shards if whole_tiles and one_row and powers else plain_shards)(*arrays)
+
+    return jax.shard_map(body, mesh=mesh, in_specs=in_specs, out_specs=out_specs, check_vma=False)

time: 550 us -> 162 us (0.29); the launches traced: 540 us -> 162 us
  waiting for transfers between devices: 280 us -> 0 us
  Pallas kernels: 0 us -> 159 us
  matrix products: 95.8 us -> 0 us
  blocking collectives: 80.4 us -> 0 us
  local copies, waits for them, and re-layouts: 35.4 us -> 0 us
  other arithmetic: 28 us -> 0 us
  between operations: 20.3 us -> 2.13 us
    reduce_scatter x4 -> x0, waiting for transfers between devices: 258 us -> none  [the longest x1 100 us: shards(): lax.psum_scatter(down_weight_grad, 'dp', scatter_dimension=0, tiled=True)]
    pallas_call x0 -> x2, Pallas kernels: none -> 159 us  [the longest x1 157 us: layer(): pl.pallas_call(functools.partial(layer_kernel, ring, slots, dp_size), out...]
    dot_general x18 -> x0, matrix products: 95.8 us -> none  [the longest x4 26.6 us: outer_product(): lax.dot_general(left, right, (((0,), (0,)), ((), ())), preferred_element_...]
    psum x2 -> x0, blocking collectives: 52.9 us -> none  [the longest x1 42 us: shards(): totals = lax.psum(count_terms, ('group', 'dp'))]
    unnamed x1 -> x0, blocking collectives: 27.5 us -> none
    unnamed x122 -> x0, local copies, waits for them, and re-layouts: 22.6 us -> none
    psum x1 -> x0, waiting for transfers between devices: 21.9 us -> none  [shards(): summed = lax.psum(tuple(shares), 'group')]
    reduce_sum x8 -> x0, other arithmetic: 11.4 us -> none  [the longest x1 3.73 us: one_block(): row_total = jnp.sum(raised, axis=-1, keepdims=True)]
  transfers between devices with their start and end apart: 5 -> 0, of which waited for: 4 -> 0; matrix products, arithmetic and copies ran while one was open for 17% -> 0% of each run, Pallas kernels for 0% -> 0%
where the time goes in v1:
time: 162 us
  Pallas kernels  159 us (98%)
  between operations  2.13 us (1%)
    pallas_call x1, Pallas kernels, layer(): pl.pallas_call(functools.partial(layer_kernel, ring, slots, dp_size), out...  157 us

profile of v1, /device:TPU:0, one launch (start us, length us, event | category | flops | bytes accessed | tf_op | source)
XLA Modules:
  0.0 161.5 jit_solution(8384918524891729989)
XLA Ops:
  1.9 156.6 %shard_map.289 = (bf16[512,768]{1,0:T(8,128)(2,1)S(1)}, f32[512,768]{1,0:T(8,128)S(1)}, f32[36,2,12,8,128]{4,3,2,1,0:T(8,128)S(1)}, f32[72,128]{1,0:T(8,128)S(1)}) custom-call(bf16[512,768]{1,0:T(8,128)(2,1)} %bitcast.8, bf16[512,768]{1,0:T(8,128)(2,1)} %bitcast.9, s32[1]{0:T(128)S(6)} %copy.33.refs_2_, s32[1]{0:T(128)S(6)} %copy.34.refs_3_, ...), custom_call_target="tpu_custom_call" | custom-call | tf_op jit(solution)/shard_map/pallas_call | solution.py:851
  158.6 2.7 %shard_map.290 = (bf16[512,768]{1,0:T(8,128)(2,1)}, f32[512,768]{1,0:T(8,128)}, f32[12,8,2304]{2,1,0:T(8,128)}, f32[12,8,768]{2,1,0:T(8,128)}, f32[12,8,3072]{2,...) custom-call(bf16[512,768]{1,0:T(8,128)(2,1)S(1)} %get-tuple-element., ...), custom_call_target="tpu_custom_call" | custom-call | tf_op jit(solution)/shard_map/pallas_call | solution.py:971

commit v2 on v1

--- a/solution.py
+++ b/solution.py
@@ -466,23 +466,24 @@
     group = lax.axis_index("group")
     row = group * dp_size + lax.axis_index("dp")
     row_blocks = [slice(at, at + ROWS_AT_ONCE) for at in range(0, token_count, ROWS_AT_ONCE)]
-    for rows in row_blocks:
-        centered, rstd = moments(tokens_ref[rows, :].astype(f32))
-        norm1_ref[rows, :] = (centered * rstd * gain1_ref[...] + shift1_ref[...]).astype(bf16)
-
     used = jnp.where((group >= group_half) | (row < replay_ref[0]), 1.0, 0.0)
     live = mask_ref[...].astype(f32) * used
     side = lax.div(group, group_half)
     tile_rows = lax.broadcasted_iota(jnp.int32, (SUBLANES, LANES), 0)
     small_send[0] = jnp.where(tile_rows == side, jnp.sum(live, axis=1, keepdims=True), 0.0)
     loads[0].wait()
-    for third, bias in enumerate((query_bias_ref, None, value_bias_ref)):
-
-        columns = slice(third * width, (third + 1) * width)
-        product = plain_product(norm1_ref[...], proj_ref[:, columns])
-        if bias is not None:
-            product = product + bias[...]
-        heads_ref[:, columns] = product.astype(bf16)
+    row_halves = [row_blocks[: len(row_blocks) // 2], row_blocks[len(row_blocks) // 2 :]]
+    for row_half in row_halves:
+        for rows in row_half:
+            centered, rstd = moments(tokens_ref[rows, :].astype(f32))
+            norm1_ref[rows, :] = (centered * rstd * gain1_ref[...] + shift1_ref[...]).astype(bf16)
+        half = slice(row_half[0].start, row_half[-1].stop)
+        for third, bias in enumerate((query_bias_ref, None, value_bias_ref)):
+            columns = slice(third * width, (third + 1) * width)
+            product = plain_product(norm1_ref[half, :], proj_ref[:, columns])
+            if bias is not None:
+                product = product + bias[...]
+            heads_ref[half, columns] = product.astype(bf16)
 
     pl.semaphore_wait(barrier, turns)
 
@@ -551,15 +552,16 @@
 
     loads[1].wait()
 
-    product = plain_product(mixed_ref[...], out_ref[...]) + out_bias_ref[...]
-    residual_ref[...] = tokens_ref[...].astype(f32) + product
+    for row_half in row_halves:
+        half = slice(row_half[0].start, row_half[-1].stop)
+        product = plain_product(mixed_ref[half, :], out_ref[...]) + out_bias_ref[...]
+        residual_ref[half, :] = tokens_ref[half, :].astype(f32) + product
+        for rows in row_half:
+            centered, rstd = moments(residual_ref[rows, :])
+            low = (centered * rstd * gain2_ref[...] + shift2_ref[...]).astype(bf16)
+            norm2_ref[rows, :] = low
+            turned_ref[:, rows] = low.T
     count_turn(4)
-
-    for rows in row_blocks:
-        centered, rstd = moments(residual_ref[rows, :])
-        low = (centered * rstd * gain2_ref[...] + shift2_ref[...]).astype(bf16)
-        norm2_ref[rows, :] = low
-        turned_ref[:, rows] = low.T
 
     for turn in range(5, turns + 1):
         count_turn(turn)

time: 162 us -> 162 us (level)
  no operation moved by 1% of the time
where the time goes in v2:
time: 162 us
  Pallas kernels  160 us (99%)
  between operations  2.11 us (1%)
    pallas_call x1, Pallas kernels, layer(): pl.pallas_call(functools.partial(layer_kernel, ring, slots, dp_size), out...  157 us

profile of v2, /device:TPU:0, one launch (start us, length us, event | category | flops | bytes accessed | tf_op | source)
XLA Modules:
  0.0 161.7 jit_solution(7757778627062553683)
XLA Ops:
  1.9 156.9 %shard_map.289 = (bf16[512,768]{1,0:T(8,128)(2,1)S(1)}, f32[512,768]{1,0:T(8,128)S(1)}, f32[36,2,12,8,128]{4,3,2,1,0:T(8,128)S(1)}, f32[72,128]{1,0:T(8,128)S(1)}) custom-call(bf16[512,768]{1,0:T(8,128)(2,1)} %bitcast.8, bf16[512,768]{1,0:T(8,128)(2,1)} %bitcast.9, s32[1]{0:T(128)S(6)} %copy.33.refs_2_, s32[1]{0:T(128)S(6)} %copy.34.refs_3_, ...), custom_call_target="tpu_custom_call" | custom-call | tf_op jit(solution)/shard_map/pallas_call | solution.py:853
  158.8 2.7 %shard_map.290 = (bf16[512,768]{1,0:T(8,128)(2,1)}, f32[512,768]{1,0:T(8,128)}, f32[12,8,2304]{2,1,0:T(8,128)}, f32[12,8,768]{2,1,0:T(8,128)}, f32[12,8,3072]{2,...) custom-call(bf16[512,768]{1,0:T(8,128)(2,1)S(1)} %get-tuple-element., ...), custom_call_target="tpu_custom_call" | custom-call | tf_op jit(solution)/shard_map/pallas_call | solution.py:973
